TPU v7x, 256 devices: a whole 4x4x8 slice. The times are simulated.
256 devices in a mesh: kvp: 32 (over x, y, core), tp: 8 (over z).
Axes of the slice: x: 4, y: 4, z: 8, core: 2. Of those that a mesh axis runs over, the one named last changes fastest.
Arguments:
- residual: bfloat16 [8, 16384], P(None, ('kvp', 'tp')), may hold values from -10 to 10
- norm_gain: bfloat16 [16384], P(('kvp', 'tp')), may hold values from 0.25 to 1.75
- queries: bfloat16 [8, 128, 128], P(None, 'tp'), may hold values from -100 to 100
- keys: bfloat16 [8, 4096, 8, 128], P(None, 'kvp', 'tp'), may hold values from -4 to 4
- values: bfloat16 [8, 4096, 8, 128], P(None, 'kvp', 'tp'), may hold values from -12 to 12
- new_kv: bfloat16 [8, 2, 8, 128], P(None, None, 'tp'), may hold values from -8 to 8
- lens: int32 [8], replicated, may hold values from 2 to 4096, as said below
- out_weight: bfloat16 [16384, 16384], P('tp', 'kvp'), may hold values from -0.09375 to 0.09375
- gate_weight: bfloat16 [26624, 16384], P(('kvp', 'tp')), may hold values from -0.046875 to 0.046875
- up_weight: bfloat16 [26624, 16384], P(('kvp', 'tp')), may hold values from -0.046875 to 0.046875
- down_weight: bfloat16 [26624, 16384], P(('kvp', 'tp')), may hold values from -0.15625 to 0.15625
Outputs:
- layer_out: bfloat16 [8, 16384], P(None, ('kvp', 'tp'))
Inputs may be any that keep to these rules, and one draw needn't show every extreme that they name: `lens`: one request has exactly 4096 positions in use.
All inputs are finite; a program needn't handle non-finite values.
Results may differ from a plain program's by a relative error of at most 0.02.
Values may be sent and summed in bfloat16 or wider, within the bound.
A program may use at most 64 MiB of HBM per device.

v0:
```python
from functools import partial
import math

import jax
import jax.numpy as jnp
from jax import lax
from jax.sharding import PartitionSpec as P

D = 16384


eps = 1e-05
empty_score = -1e30


def joined(value, axis, join):
    pieces = jax.tree.map(lambda part: lax.all_gather(part, axis), value)
    head = jax.tree.map(lambda part: part[0], pieces)
    tail = jax.tree.map(lambda part: part[1:], pieces)
    total, _ = lax.scan(lambda total, slab: (join(total, slab), None), head, tail)
    return total


def join_parts(earlier, later):
    joint_peak = jnp.maximum(earlier[0], later[0])
    left_factor = jnp.exp(earlier[0] - joint_peak)
    right_factor = jnp.exp(later[0] - joint_peak)
    totals = earlier[1] * left_factor + later[1] * right_factor
    summed = earlier[2] * left_factor[..., None] + later[2] * right_factor[..., None]
    return (joint_peak, totals, summed)


def project_pair(totals, piece, start, gate_weight, up_weight):
    contract = (((1,), (1,)), ((), ()))
    gate_part = lax.dot_general(piece, gate_weight, contract, preferred_element_type=jnp.float32)
    up_part = lax.dot_general(piece, up_weight, contract, preferred_element_type=jnp.float32)
    return (gate_part, up_part)


def local(
    residual,
    norm_gain,
    queries,
    keys,
    values,
    new_kv,
    lens,
    out_weight,
    gate_weight,
    up_weight,
    down_weight,
):
    batch_size, ctx_local, kv_local, head_dim = keys.shape
    heads_local = queries.shape[1]
    group_size = heads_local // kv_local
    score_scale = 1.0 / math.sqrt(head_dim)
    positions = lax.axis_index("kvp") * ctx_local + jnp.arange(ctx_local, dtype=jnp.int32)
    visible_mask = (positions[None, :] < lens[:, None])[:, None, None, :]
    grouped = queries.reshape(batch_size, kv_local, group_size, head_dim)
    scores = (
        jnp.einsum("bgqd,bcgd->bgqc", grouped, keys, preferred_element_type=jnp.float32)
        * score_scale
    )
    scores = jnp.where(visible_mask, scores, empty_score)
    local_peak = jnp.max(scores, axis=-1)
    weights = jnp.where(visible_mask, jnp.exp(scores - local_peak[..., None]), 0.0)
    local_total = jnp.sum(weights, axis=-1)
    local_sum = jnp.einsum(
        "bgqc,bcgd->bgqd", weights, values.astype(jnp.float32), precision=lax.Precision.HIGHEST
    )
    cache_peak, cache_total, cache_sum = joined(
        (local_peak, local_total, local_sum), "kvp", join_parts
    )
    fresh = (
        jnp.einsum("bgqd,bgd->bgq", grouped, new_kv[:, 0], preferred_element_type=jnp.float32)
        * score_scale
    )
    top_score = jnp.maximum(cache_peak, fresh)
    old_factor = jnp.exp(cache_peak - top_score)
    fresh_weight = jnp.exp(fresh - top_score)
    totals = cache_total * old_factor + fresh_weight
    summed = (
        cache_sum * old_factor[..., None]
        + fresh_weight[..., None] * new_kv[:, 1].astype(jnp.float32)[:, :, None, :]
    )
    attended = (
        (summed / totals[..., None])
        .reshape(batch_size, heads_local * head_dim)
        .astype(jnp.bfloat16)
    )
    partial_proj = jnp.dot(attended, out_weight, preferred_element_type=jnp.float32)
    ff_local = gate_weight.shape[0]
    empty = jnp.zeros((batch_size, ff_local), jnp.float32)
    folder = partial(project_pair, gate_weight=gate_weight, up_weight=up_weight)
    proj_slice = lax.psum_scatter(partial_proj, "tp", scatter_dimension=1, tiled=True)
    hidden_state = (residual.astype(jnp.float32) + proj_slice).astype(jnp.bfloat16)
    hidden_float = hidden_state.astype(jnp.float32)
    square_total = lax.psum(jnp.sum(hidden_float * hidden_float, axis=-1), ("kvp", "tp"))
    inverse = lax.rsqrt(square_total / D + eps)
    scaled = (hidden_float * inverse[:, None] * norm_gain.astype(jnp.float32)).astype(jnp.bfloat16)
    gate, upward = folder(
        (empty, empty), lax.all_gather(scaled, ("kvp", "tp"), axis=1, tiled=True), jnp.int32(0)
    )
    inner = (jax.nn.silu(gate) * upward).astype(jnp.bfloat16)
    feed_terms = jnp.dot(inner, down_weight, preferred_element_type=jnp.float32)
    feed_out = lax.psum_scatter(feed_terms, ("kvp", "tp"), scatter_dimension=1, tiled=True)
    return (hidden_state.astype(jnp.float32) + feed_out).astype(jnp.bfloat16)


def solution(mesh):
    in_specs = (
        P(None, ("kvp", "tp")),
        P(("kvp", "tp")),
        P(None, "tp", None),
        P(None, "kvp", "tp", None),
        P(None, "kvp", "tp", None),
        P(None, None, "tp", None),
        P(),
        P("tp", "kvp"),
        P(("kvp", "tp"), None),
        P(("kvp", "tp"), None),
        P(("kvp", "tp"), None),
    )
    out_specs = P(None, ("kvp", "tp"))
    return jax.shard_map(local, mesh=mesh, in_specs=in_specs, out_specs=out_specs, check_vma=False)
```

profile of v0, /device:TPU:1, one launch (start us, length us, event | category | flops | bytes accessed | tf_op | source)
XLA Modules:
  0.0 1614.2 jit_solution(15982186245943111191)
XLA Ops:
  7.4 1.4 fusion.36
  8.8 2.0 fusion.7
  11.7 26.2 %all-gather = f32[256,16]{1,0:T(8,128)S(1)} all-gather(f32[8,16]{1,0:T(8,128)S(1)} %get-tuple-element.93), channel_id=2, replica_groups=mesh['kvp'=32,'tp'=8] {'kvp'}, dimensions={0}, use_global_device_ids=true | all-gather | bytes 16896 | tf_op jit(solution)/shard_map/all_gather | solution.py:17
  38.1 24.0 %all-gather.1 = f32[256,16]{1,0:T(8,128)S(1)} all-gather(f32[8,16]{1,0:T(8,128)S(1)} %fusion.10), channel_id=3, replica_groups=mesh['kvp'=32,'tp'=8] {'kvp'}, dimensions={0}, use_global_device_ids=true | all-gather | bytes 16896 | tf_op jit(solution)/shard_map/all_gather | solution.py:17
  65.1 3.0 slice.43
  68.1 73.4 %while.14 = (s32[]{:T(128)}, f32[8,1,16]{2,0,1:T(8,128)S(1)}, f32[8,1,16]{2,0,1:T(8,128)S(1)}, f32[8,1,16,128]{3,2,1,0:T(8,128)S(1)}, f32[31,8,1,16]{3,1,2,0:T(8...) while((s32[]{:T(128)}, f32[8,1,16]{2,0,1:T(8,128)S(1)}, ...), condition=%wide.region_3.4_spmd, body=%wide.region_2.3_spmd.sunk | while | flops 50050 | bytes 204393 | solution.py:20
  69.5 1.0 fusion.51
  71.9 1.0 fusion.51
  74.3 1.0 fusion.51
  76.6 1.0 fusion.51
  79.0 1.0 fusion.51
  81.4 1.0 fusion.51
  83.8 1.0 fusion.51
  86.1 1.0 fusion.51
  88.5 1.0 fusion.51
  107.4 1.0 fusion.51
  141.7 3.2 convolution_bitcast_fusion.1
  145.0 30.7 %reduce-scatter.7.cloned.1.call-done = f32[64,8]{1,0:T(8,128)} async-done(((f32[512,8]{1,0:T(8,128)}), f32[64,8]{1,0:T(8,128)}) %reduce-scatter.7.cloned.1.call-update) | async-done | bytes 2064
  176.7 80.2 %psum.7 = f32[8]{0:T(128)S(1)} all-reduce(f32[8]{0:T(128)S(1)} %get-tuple-element.84), channel_id=1, replica_groups=mesh['kvp'=32,'tp'=8] {'kvp','tp'}, use_global_device_ids=true, to_apply=%region_6.7 | all-reduce | flops 8 | bytes 64 | tf_op jit(solution)/shard_map/psum | solution.py:98
  257.0 68.3 %all-gather.3 = bf16[256,64,8]{1,2,0:T(8,128)(2,1)S(1)} all-gather(bf16[1,64,8]{1,2,0:T(8,128)(2,1)S(1)} %fusion.30), channel_id=1, replica_groups=mesh['kvp'=32,'tp'=8] {'kvp','tp'}, dimensions={0}, use_global_device_ids=true | all-gather | bytes 263168 | tf_op jit(solution)/shard_map/all_gather | solution.py:102
  326.1 2.2 reshape.122
  328.3 3.0 fusion.37
  331.4 9.2 convolution_bitcast_fusion
  340.6 1265.6 %reduce-scatter.9.cloned.1.call-done = f32[64,8]{1,0:T(8,128)} async-done(((f32[16384,8]{1,0:T(8,128)}), f32[64,8]{1,0:T(8,128)}) %reduce-scatter.9.cloned.1.call-update) | async-done | bytes 2064
  (148 shorter events, 71.5 us)
Async XLA Ops:
  6.5 324.8 %copy-start = (bf16[104,16384]{1,0:T(8,128)(2,1)S(1)}, bf16[104,16384]{1,0:T(8,128)(2,1)}, u32[]{:S(2)}) copy-start(bf16[104,16384]{1,0:T(8,128)(2,1)} %param.23) | copy-start | bytes 10223620
  6.5 57.7 %all-gather.6.cloned.1.call-start = ((), (), s32[]{:S(2)}) async-start(), calls=%async_computation.2 | async-start | bytes 2162688 | tf_op jit(solution)/shard_map/all_gather | solution.py:17
  10.9 164.9 %reduce-scatter.7.cloned.1.call-start = ((), (), s32[]{:S(2)}) async-start(), calls=%async_computation.3 | async-start | bytes 294912
  65.1 79.9 %copy-start.2 = (bf16[64]{0:T(256)(128)(2,1)S(1)}, bf16[64]{0:T(256)(128)(2,1)}, u32[]{:S(2)}) copy-start(bf16[64]{0:T(256)(128)(2,1)} %param.14) | copy-start | bytes 388
  65.1 111.4 %copy-start.1 = (bf16[8,64]{1,0:T(8,128)(2,1)S(1)}, bf16[8,64]{1,0:T(8,128)(2,1)}, u32[]{:S(2)}) copy-start(bf16[8,64]{1,0:T(8,128)(2,1)} %param.13) | copy-start | bytes 3076
  144.9 1461.3 %reduce-scatter.9.cloned.1.call-start = ((), (), s32[]{:S(2)}) async-start(), calls=%async_computation.4 | async-start | bytes 8421376
Sparse Core Ops, SparseCore 0:
  11.0 53.0 all-gather.5
  145.1 30.6 reduce-scatter.6
  340.8 1265.4 reduce-scatter.8
where the time goes:
time: 1630 us; the launch traced here: 1610 us
  waiting for transfers between devices  1300 us (80%)
  blocking collectives  199 us (12%)
  other arithmetic  75.4 us (5%)
  matrix products  19.8 us (1%)
    unnamed x5, waiting for transfers between devices  1300 us
    psum x1, blocking collectives, local(): lax.psum(jnp.sum(hidden_float * hidden_float, axis=-1), ('kvp', 'tp'))  80.2 us
    all_gather x1, blocking collectives, local(): lax.all_gather(scaled, ('kvp', 'tp'), axis=1, tiled=True)  68.3 us
    all_gather x2, blocking collectives, joined(): pieces = jax.tree.map(lambda part: lax.all_gather(part, axis), value)  50.2 us
  transfers between devices with their start and end apart: 3, of which 2 were waited for; matrix products, arithmetic and copies ran while one was open for 0% of the time, Pallas kernels for 0%

commit v1 on v0

v1 whole, which is shorter than its diff:
```python
import functools
import math

import jax
import jax.numpy as jnp
from jax import lax
from jax.experimental import pallas as pl
from jax.experimental.pallas import tpu as pltpu
from jax.sharding import PartitionSpec as P

MESH = pl.DeviceIdType.MESH
BF = jnp.bfloat16
F32 = jnp.float32
D = 16384
EPS = 1e-05
EMPTY = -1e30
X, Y, C, Z = 4, 4, 2, 8
KVP = X * Y * C


def hops(dx, dy):
    return min(dx, X - dx) + min(dy, Y - dy)


ROW = sorted([(dx, 0, dc) for dx in range(X) for dc in range(C)][1:], key=lambda o: -hops(o[0], o[1]))
COL = sorted([(0, dy, dc) for dy in range(Y) for dc in range(C)][1:], key=lambda o: -hops(o[0], o[1]))
PLANE = sorted(
    [(dx, dy, dc) for dx in range(X) for dy in range(Y) for dc in range(C)][1:],
    key=lambda o: (-hops(o[0], o[1]), -o[2]),
)
DEPTH = sorted(range(1, Z), key=lambda dz: -min(dz, Z - dz))


def pack(ref, o, m, l):
    rows = lax.broadcasted_iota(jnp.int32, (16, 128), 0)
    high = l.astype(BF).astype(F32)
    tail = jnp.where(rows == 0, m, jnp.where(rows == 1, high, jnp.where(rows == 2, l - high, 0.0)))
    ref[pl.ds(0, 64), :] = o.astype(BF)
    ref[pl.ds(64, 16), :] = tail.astype(BF)


def unpack(x):
    o = x[0:64].astype(F32)
    tail = x[64:80].astype(F32)
    return o, tail[0:1], tail[1:2] + tail[2:3]


def combine(parts):
    m = functools.reduce(jnp.maximum, [p[1] for p in parts])
    o, l = 0.0, 0.0
    for po, pm, pl_ in parts:
        factor = jnp.exp(pm - m)
        o = o + po * factor
        l = l + pl_ * factor
    return o, m, l


def kernel(
    res_h, gain_h, q_h, k_h, v_h, nkv_h, lens_h, ow_h, gw_h, uw_h, dw_h,
    out_ref,
    res_v, gain_v, q_v, k_v, v_v, nkv_v, lens_s, ow_v, gw_v, uw_v, dw_v,
    row_send, row_recv, col_send, col_recv, side_send, side_recv,
    proj_send, proj_recv, norm_send, norm_recv, down_send, down_recv, last_send, last_recv,
    load_sem, send_sem, recv_sem, norm_sem,
):
    kvp = lax.axis_index("kvp")
    z = lax.axis_index("tp")
    x = kvp // (Y * C)
    y = lax.rem(kvp // C, Y)
    c = lax.rem(kvp, C)
    xs = [x] + [lax.rem(x + d, X) for d in range(1, X)]
    ys = [y] + [lax.rem(y + d, Y) for d in range(1, Y)]
    cs = [c, 1 - c]
    zs = [z] + [lax.rem(z + d, Z) for d in range(1, Z)]

    def index(o):
        return (xs[o[0]] * Y + ys[o[1]]) * C + cs[o[2]]

    def origin(o):
        return index(((X - o[0]) % X, (Y - o[1]) % Y, (C - o[2]) % C))

    small = [(k_h, k_v), (q_h, q_v), (v_h, v_v), (nkv_h, nkv_v), (lens_h, lens_s), (res_h, res_v), (gain_h, gain_v)]
    large = [(ow_h, ow_v), (gw_h, gw_v), (uw_h, uw_v), (dw_h, dw_v)]
    small = [pltpu.make_async_copy(s, d, load_sem.at[i]) for i, (s, d) in enumerate(small)]
    large = [pltpu.make_async_copy(s, d, load_sem.at[7 + i]) for i, (s, d) in enumerate(large)]
    for copy in small:
        copy.start()

    barrier = pltpu.get_barrier_semaphore()
    for dz in DEPTH:
        pl.semaphore_signal(barrier, inc=1, device_id=(kvp, zs[dz]), device_id_type=MESH)
    for o in PLANE:
        pl.semaphore_signal(barrier, inc=1, device_id=(index(o), z), device_id_type=MESH)

    for copy in small:
        copy.wait()
    for copy in large:
        copy.start()

    scale = 1.0 / math.sqrt(128)
    ri = lax.broadcasted_iota(jnp.int32, (128, 128), 0)
    li = lax.broadcasted_iota(jnp.int32, (128, 128), 1)
    perm = (li == (ri & 7) * 16 + (ri >> 3)).astype(BF)
    q = jnp.dot(perm, q_v[...].reshape(128, 128), preferred_element_type=F32)
    qm = jnp.concatenate([jnp.where((ri & 7) == b, q, 0.0).astype(BF) for b in range(8)], axis=1)
    kc = jnp.concatenate([k_v[b] for b in range(8)], axis=1)
    nkv = nkv_v[...].astype(F32)
    nk = nkv[:, 0, :]
    nv = nkv[:, 1, :]
    nkc = jnp.concatenate([jnp.broadcast_to(nk[b : b + 1], (8, 128)) for b in range(8)], axis=1).astype(BF)
    contract = (((1,), (1,)), ((), ()))
    s = lax.dot_general(kc, qm, contract, preferred_element_type=F32) * scale
    fresh = lax.dot_general(nkc, qm, contract, preferred_element_type=F32)[0:1] * scale
    lane = lax.broadcasted_iota(jnp.int32, (1, 128), 1) & 7
    limit = functools.reduce(lambda a, b: jnp.where(lane == b, lens_s[b], a), range(1, 8), jnp.full((1, 128), lens_s[0]))
    live = (ri + kvp * 128) < limit
    mine = (jnp.zeros((1, 128), jnp.int32) + kvp) == 0
    s = jnp.where(live, s, EMPTY)
    fresh = jnp.where(mine, fresh, EMPTY)
    m = jnp.maximum(jnp.max(s, axis=0, keepdims=True), fresh)
    m = m.astype(BF).astype(F32)
    p = jnp.where(live, jnp.exp(s - m), 0.0)
    pf = jnp.where(mine, jnp.exp(fresh - m), 0.0)
    l = jnp.sum(p, axis=0, keepdims=True) + pf
    pm = jnp.concatenate([jnp.where((li & 7) == b, p, 0.0).astype(BF) for b in range(8)], axis=0)
    vt = jnp.concatenate([v_v[b].T for b in range(8)], axis=1)
    o = jnp.dot(vt, pm, preferred_element_type=F32)
    ri8 = lax.broadcasted_iota(jnp.int32, (8, 128), 0)
    li8 = lax.broadcasted_iota(jnp.int32, (8, 128), 1)
    pfm = jnp.where((li8 & 7) == ri8, pf, 0.0)
    pad = jnp.zeros((120, 128), F32)
    nvt = jnp.concatenate([nv, pad], axis=0).T.astype(BF)
    o = o + jnp.dot(nvt, jnp.concatenate([pfm, pad], axis=0).astype(BF), preferred_element_type=F32)
    pack(row_send.at[0], o[0:64], m, l)
    pack(row_send.at[1], o[64:128], m, l)
    side_send[...] = jnp.concatenate(
        [res_v[...], jnp.broadcast_to(gain_v[...].astype(F32).reshape(1, 64), (8, 64)).astype(BF)], axis=1
    )

    pl.semaphore_wait(barrier, len(PLANE) + len(DEPTH))

    def send(src, dst, sends, recvs, device):
        pltpu.make_async_remote_copy(src, dst, sends, recvs, device_id=device, device_id_type=MESH).start()

    def whole(ref, sem):
        pltpu.make_async_copy(ref, ref, sem).wait()

    for j, o_ in enumerate(ROW):
        send(row_send.at[cs[o_[2]]], row_recv.at[j], send_sem.at[0], recv_sem.at[0], (index(o_), z))
    for j, dz in enumerate(DEPTH):
        send(side_send, side_recv.at[j], send_sem.at[1], recv_sem.at[1], (kvp, zs[dz]))
    whole(row_recv, recv_sem.at[0])
    o, m, l = combine([unpack(row_send[c])] + [unpack(row_recv[j]) for j in range(len(ROW))])
    pack(col_send, o, m, l)

    for j, o_ in enumerate(COL):
        send(col_send, col_recv.at[j], send_sem.at[2], recv_sem.at[2], (index(o_), z))
    whole(side_recv, recv_sem.at[1])
    lane8 = lax.broadcasted_iota(jnp.int32, (8, 128), 1)
    low = lane8 < 64
    side = [side_send[...].astype(F32)] + [side_recv[j].astype(F32) for j in range(Z - 1)]
    owner = [z] + [zs[Z - dz] for dz in DEPTH]
    res_parts, gain_parts = [], []
    for g in range(Z // 2):
        r, gn = jnp.zeros((8, 128), F32), jnp.zeros((8, 128), F32)
        for t, own in zip(side, owner):
            turned = pltpu.roll(t, 64, 1)
            here = (jnp.zeros((8, 128), jnp.int32) + own) == jnp.where(low, 2 * g, 2 * g + 1)
            r = jnp.where(here, jnp.where(low, t, turned), r)
            gn = jnp.where(here, jnp.where(low, turned, t), gn)
        res_parts.append(r)
        gain_parts.append(gn)
    res = jnp.concatenate(res_parts, axis=1)
    gain = jnp.concatenate(gain_parts, axis=1)
    whole(col_recv, recv_sem.at[2])
    own = [unpack(col_send[...])] + [unpack(col_recv[j]) for j, o_ in enumerate(COL) if o_[2] == 0]
    other = [unpack(col_recv[j]) for j, o_ in enumerate(COL) if o_[2] == 1]
    o, _, l = combine(own)
    own = o / l
    o, _, l = combine(other)
    other = o / l
    first = (jnp.zeros((64, 128), jnp.int32) + c) == 0
    att = jnp.concatenate([jnp.where(first, own, other), jnp.where(first, other, own)], axis=0).T
    att = jnp.concatenate([att[8 * h : 8 * h + 8] for h in range(16)], axis=1).astype(BF)

    large[0].wait()
    part = jnp.dot(att, ow_v[...], preferred_element_type=F32)
    proj_send[...] = part.astype(BF)
    for j, dz in enumerate(DEPTH):
        send(proj_send, proj_recv.at[j], send_sem.at[3], recv_sem.at[3], (kvp, zs[dz]))
    whole(proj_recv, recv_sem.at[3])
    total = part
    for j in range(Z - 1):
        total = total + proj_recv[j].astype(F32)
    hidden = (res + total).astype(BF).astype(F32)
    square = jnp.sum(hidden * hidden, axis=1, keepdims=True)
    high = square.astype(BF).astype(F32)
    norm_send[:, pl.ds(0, 512)] = (hidden * gain).astype(BF)
    norm_send[:, pl.ds(512, 128)] = jnp.where(low, high, square - high).astype(BF)

    for j, o_ in enumerate(PLANE):
        send(norm_send, norm_recv.at[j], send_sem.at[4], norm_sem.at[j], (index(o_), z))
    for copy in large[1:3]:
        copy.wait()

    def gate_up(ref, block, gate, up):
        feats = ref[:, pl.ds(0, 512)]
        cols = pl.ds(pl.multiple_of(block * 512, 512), 512)
        gate = gate + lax.dot_general(feats, gw_v[:, cols], contract, preferred_element_type=F32)
        up = up + lax.dot_general(feats, uw_v[:, cols], contract, preferred_element_type=F32)
        return gate, up, ref[:, pl.ds(512, 128)].astype(F32)

    gate = jnp.zeros((8, 104), F32)
    up = jnp.zeros((8, 104), F32)
    gate, up, squares = gate_up(norm_send, kvp, gate, up)
    for j in reversed(range(len(PLANE))):
        slot = norm_recv.at[j]
        whole(slot, norm_sem.at[j])
        gate, up, extra = gate_up(slot, origin(PLANE[j]), gate, up)
        squares = squares + extra
    squares = squares[:, 0:1] + squares[:, 64:65]
    inverse = lax.rsqrt(squares * (1.0 / D) + EPS)
    gate = gate * inverse
    up = up * inverse
    inner = (gate / (1.0 + jnp.exp(-gate)) * up).astype(BF)

    large[3].wait()

    def down(block):
        cols = pl.ds(pl.multiple_of(block * 512, 512), 512)
        return jnp.dot(inner, dw_v[:, cols], preferred_element_type=F32)

    for j, o_ in enumerate(PLANE):
        down_send[j] = down(index(o_)).astype(BF)
        send(down_send.at[j], down_recv.at[j], send_sem.at[5], recv_sem.at[4], (index(o_), z))
    total = down(kvp)
    whole(down_recv, recv_sem.at[4])
    for j in range(len(PLANE)):
        total = total + down_recv[j].astype(F32)

    for g in range(Z // 2):
        last_send[g] = total[:, 128 * g : 128 * g + 128]
    for j, dz in enumerate(DEPTH):
        send(last_send.at[zs[dz] // 2], last_recv.at[j], send_sem.at[6], recv_sem.at[5], (kvp, zs[dz]))
    mine = last_send[z // 2]
    hid = jnp.zeros((8, 128), F32)
    for g in range(Z // 2):
        hid = jnp.where((jnp.zeros((8, 128), jnp.int32) + z // 2) == g, hidden[:, 128 * g : 128 * g + 128], hid)
    whole(last_recv, recv_sem.at[5])
    for j in range(Z - 1):
        mine = mine + last_recv[j]
    mine = mine + hid
    odd = (jnp.zeros((8, 128), jnp.int32) + lax.rem(z, 2)) == 1
    mine = jnp.where(odd, pltpu.roll(mine, 64, 1), mine)
    out_ref[...] = mine[:, 0:64].astype(BF)

    for i, ref in enumerate((row_recv, side_recv, col_recv, proj_recv, norm_recv, down_recv, last_recv)):
        whole(ref, send_sem.at[i])


def local(residual, norm_gain, queries, keys, values, new_kv, lens, out_weight, gate_weight, up_weight, down_weight):
    V = pltpu.VMEM
    n = len(PLANE)
    scratch = [
        V((8, 64), BF), V((64,), BF), V((8, 16, 128), BF), V((8, 128, 128), BF), V((8, 128, 128), BF),
        V((8, 2, 128), BF), pltpu.SMEM((8,), jnp.int32), V((2048, 512), BF),
        V((104, D), BF), V((104, D), BF), V((104, D), BF),
        V((2, 80, 128), BF), V((7, 80, 128), BF), V((80, 128), BF), V((7, 80, 128), BF),
        V((8, 128), BF), V((7, 8, 128), BF),
        V((8, 512), BF), V((7, 8, 512), BF), V((8, 640), BF), V((n, 8, 640), BF),
        V((n, 8, 512), BF), V((n, 8, 512), BF), V((4, 8, 128), F32), V((7, 8, 128), F32),
        pltpu.SemaphoreType.DMA((11,)), pltpu.SemaphoreType.DMA((7,)), pltpu.SemaphoreType.DMA((6,)),
        pltpu.SemaphoreType.DMA((n,)),
    ]
    return pl.pallas_call(
        kernel,
        name="decode_step",
        out_shape=jax.ShapeDtypeStruct((8, 64), BF),
        in_specs=[pl.BlockSpec(memory_space=pl.ANY)] * 11,
        out_specs=pl.BlockSpec(memory_space=pltpu.VMEM),
        scratch_shapes=scratch,
        cost_estimate=pl.CostEstimate(flops=120_000_000, bytes_accessed=13_000_000, transcendentals=20_000),
        compiler_params=pltpu.CompilerParams(collective_id=0, has_side_effects=True, vmem_limit_bytes=48 << 20),
    )(
        residual, norm_gain, queries, keys.reshape(8, 128, 128), values.reshape(8, 128, 128),
        new_kv.reshape(8, 2, 128), lens, out_weight, gate_weight, up_weight, down_weight,
    )


def solution(mesh):
    in_specs = (
        P(None, ("kvp", "tp")),
        P(("kvp", "tp")),
        P(None, "tp", None),
        P(None, "kvp", "tp", None),
        P(None, "kvp", "tp", None),
        P(None, None, "tp", None),
        P(),
        P("tp", "kvp"),
        P(("kvp", "tp"), None),
        P(("kvp", "tp"), None),
        P(("kvp", "tp"), None),
    )
    out_specs = P(None, ("kvp", "tp"))
    return jax.shard_map(local, mesh=mesh, in_specs=in_specs, out_specs=out_specs, check_vma=False)
```

time: 1630 us -> 52.3 us (0.03)
  waiting for transfers between devices: 1300 us -> 0 us
  blocking collectives: 199 us -> 0 us
  other arithmetic: 75.4 us -> 0 us
  Pallas kernels: 0 us -> 42.5 us
  matrix products: 19.8 us -> 0 us
    unnamed x5 -> x0, waiting for transfers between devices: 1300 us -> none
    all_gather x3 -> x0, blocking collectives: 118 us -> none  [the longest x1 68.3 us: local(): lax.all_gather(scaled, ('kvp', 'tp'), axis=1, tiled=True)]
    psum x1 -> x0, blocking collectives: 80.2 us -> none  [local(): lax.psum(jnp.sum(hidden_float * hidden_float, axis=-1), ('kvp', 'tp'))]
    mul x64 -> x0, other arithmetic: 43.8 us -> none  [the longest x31 21.7 us: join_parts(): later[2] * right_factor[..., None]]
    pallas_call x0 -> x1, Pallas kernels: none -> 42.5 us  [local(): pl.pallas_call(kernel, name='decode_step', out_shape=jax.ShapeDtypeStruct...]
    add x32 -> x0, other arithmetic: 29.6 us -> none  [the longest x31 29.6 us: join_parts(): earlier[2] * left_factor[..., None] + later[2] * right_factor[..., None]]
  transfers between devices with their start and end apart: 3 -> 0, of which waited for: 2 -> 0; matrix products, arithmetic and copies ran while one was open for 0% -> 0% of each run, Pallas kernels for 0% -> 0%
where the time goes in v1:
time: 52.3 us; the launch traced here: 52 us
  Pallas kernels  42.5 us (81%)
  local copies, waits for them, and re-layouts  9.47 us (18%)
    pallas_call x1, Pallas kernels, local(): pl.pallas_call(kernel, name='decode_step', out_shape=jax.ShapeDtypeStruct...  42.5 us
    unnamed x19, local copies, waits for them, and re-layouts  9.47 us

profile of v1, /device:TPU:1, one launch (start us, length us, event | category | flops | bytes accessed | tf_op | source)
XLA Modules:
  0.0 52.0 jit_solution(9104763607534219512)
XLA Ops:
  0.0 0.0 copy-start
  0.0 2.0 %copy-done = bf16[104,16384]{1,0:T(8,128)(2,1)S(1)} copy-done((bf16[104,16384]{1,0:T(8,128)(2,1)S(1)}, bf16[104,16384]{1,0:T(8,128)(2,1)}, u32[]{:S(2)}) %copy-start) | copy-done | bytes 3407896
  2.0 0.0 copy-start.1
  2.0 1.6 %copy-done.1 = bf16[2048,512]{1,0:T(8,128)(2,1)S(1)} copy-done((bf16[2048,512]{1,0:T(8,128)(2,1)S(1)}, bf16[2048,512]{1,0:T(8,128)(2,1)}, u32[]{:S(2)}) %copy-start.1) | copy-done | bytes 2097176
  3.6 0.0 copy-start.2
  3.6 0.9 %copy-done.2 = bf16[8,128,1,128]{3,1,2,0:T(8,128)(2,1)S(1)} copy-done((bf16[8,128,1,128]{3,1,2,0:T(8,128)(2,1)S(1)}, bf16[8,128,1,128]{3,1,2,0:T(8,128)(2,1)}, u32[]{:S(2)}) %copy-start.2) | copy-done | bytes 262168
  4.5 0.0 copy-start.3
  4.5 0.9 %copy-done.3 = bf16[8,128,1,128]{3,1,2,0:T(8,128)(2,1)S(1)} copy-done((bf16[8,128,1,128]{3,1,2,0:T(8,128)(2,1)S(1)}, bf16[8,128,1,128]{3,1,2,0:T(8,128)(2,1)}, u32[]{:S(2)}) %copy-start.3) | copy-done | bytes 262168
  5.5 0.0 copy-start.4
  5.5 0.8 %copy-done.4 = bf16[8,16,128]{2,1,0:T(8,128)(2,1)S(1)} copy-done((bf16[8,16,128]{2,1,0:T(8,128)(2,1)S(1)}, bf16[8,16,128]{2,1,0:T(8,128)(2,1)}, u32[]{:S(2)}) %copy-start.4) | copy-done | bytes 32792
  6.2 0.0 copy-start.5
  6.2 0.7 %copy-done.5 = bf16[8,2,1,128]{3,1,2,0:T(2,128)(2,1)S(1)} copy-done((bf16[8,2,1,128]{3,1,2,0:T(2,128)(2,1)S(1)}, bf16[8,2,1,128]{3,1,2,0:T(2,128)(2,1)}, u32[]{:S(2)}) %copy-start.5) | copy-done | bytes 4120
  6.9 0.0 copy-start.6
  6.9 0.7 %copy-done.6 = bf16[8,64]{1,0:T(8,128)(2,1)S(1)} copy-done((bf16[8,64]{1,0:T(8,128)(2,1)S(1)}, bf16[8,64]{1,0:T(8,128)(2,1)}, u32[]{:S(2)}) %copy-start.6) | copy-done | bytes 1048
  7.6 0.0 copy-start.7
  7.6 0.7 %copy-done.7 = bf16[64]{0:T(256)(128)(2,1)S(1)} copy-done((bf16[64]{0:T(256)(128)(2,1)S(1)}, bf16[64]{0:T(256)(128)(2,1)}, u32[]{:S(2)}) %copy-start.7) | copy-done | bytes 152
  8.2 0.0 copy-start.8
  8.2 0.7 %copy-done.8 = s32[8]{0:T(128)S(1)} copy-done((s32[8]{0:T(128)S(1)}, s32[8]{0:T(128)}, u32[]{:S(2)}) %copy-start.8) | copy-done | bytes 56
  8.9 42.5 %decode_step.1 = bf16[8,64]{1,0:T(8,128)(2,1)S(1)} custom-call(bf16[8,64]{1,0:T(8,128)(2,1)S(1)} %copy-done.6, bf16[64]{0:T(256)(128)(2,1)S(1)} %copy-done.7, bf16[8,16,128]{2,1,0:T(8,128)(2,1)S(1)} %copy-done.4, bf16[8,128,128]{2,1,0:T(8,128)(2,1)S(1)} %bitcast.3, bf16[8,128,128]{2,1,0:T(8,128)(2,1)S(1)} %bitcast.4, bf16[8,2,128]{2,1,0:T(2,128)(2,1)S(1)} %bitcast.5, ...), custom_call_target="tpu_custom_call" | custom-call | flops 120000000 | bytes 13000000 | tf_op jit(solution)/shard_map/decode_step/pallas_call | solution.py:275
  51.4 0.6 %copy.13 = bf16[8,64]{1,0:T(8,128)(2,1)} copy(bf16[8,64]{1,0:T(8,128)(2,1)S(1)} %decode_step.1) | data formatting | bytes 2048
Async XLA Ops:
  0.0 2.0 %copy-start = (bf16[104,16384]{1,0:T(8,128)(2,1)S(1)}, bf16[104,16384]{1,0:T(8,128)(2,1)}, u32[]{:S(2)}) copy-start(bf16[104,16384]{1,0:T(8,128)(2,1)} %gw_h.1) | copy-start | bytes 10223620
  2.0 1.6 %copy-start.1 = (bf16[2048,512]{1,0:T(8,128)(2,1)S(1)}, bf16[2048,512]{1,0:T(8,128)(2,1)}, u32[]{:S(2)}) copy-start(bf16[2048,512]{1,0:T(8,128)(2,1)} %ow_h.1) | copy-start | bytes 6291460
  3.6 0.9 %copy-start.2 = (bf16[8,128,1,128]{3,1,2,0:T(8,128)(2,1)S(1)}, bf16[8,128,1,128]{3,1,2,0:T(8,128)(2,1)}, u32[]{:S(2)}) copy-start(bf16[8,128,1,128]{3,1,2,0:T(8,128)(2,1)} %param.14) | copy-start | bytes 786436
  4.5 0.9 %copy-start.3 = (bf16[8,128,1,128]{3,1,2,0:T(8,128)(2,1)S(1)}, bf16[8,128,1,128]{3,1,2,0:T(8,128)(2,1)}, u32[]{:S(2)}) copy-start(bf16[8,128,1,128]{3,1,2,0:T(8,128)(2,1)} %param.15) | copy-start | bytes 786436
  5.5 0.8 %copy-start.4 = (bf16[8,16,128]{2,1,0:T(8,128)(2,1)S(1)}, bf16[8,16,128]{2,1,0:T(8,128)(2,1)}, u32[]{:S(2)}) copy-start(bf16[8,16,128]{2,1,0:T(8,128)(2,1)} %q_h.1) | copy-start | bytes 98308
  6.2 0.7 %copy-start.5 = (bf16[8,2,1,128]{3,1,2,0:T(2,128)(2,1)S(1)}, bf16[8,2,1,128]{3,1,2,0:T(2,128)(2,1)}, u32[]{:S(2)}) copy-start(bf16[8,2,1,128]{3,1,2,0:T(2,128)(2,1)} %param.16) | copy-start | bytes 12292
  6.9 0.7 %copy-start.6 = (bf16[8,64]{1,0:T(8,128)(2,1)S(1)}, bf16[8,64]{1,0:T(8,128)(2,1)}, u32[]{:S(2)}) copy-start(bf16[8,64]{1,0:T(8,128)(2,1)} %res_h.1) | copy-start | bytes 3076
  7.6 0.7 %copy-start.7 = (bf16[64]{0:T(256)(128)(2,1)S(1)}, bf16[64]{0:T(256)(128)(2,1)}, u32[]{:S(2)}) copy-start(bf16[64]{0:T(256)(128)(2,1)} %gain_h.1) | copy-start | bytes 388
  8.2 0.7 %copy-start.8 = (s32[8]{0:T(128)S(1)}, s32[8]{0:T(128)}, u32[]{:S(2)}) copy-start(s32[8]{0:T(128)} %lens_h.1) | copy-start | bytes 100

commit v2 on v1

--- a/solution.py
+++ b/solution.py
@@ -28,6 +28,8 @@
     [(dx, dy, dc) for dx in range(X) for dy in range(Y) for dc in range(C)][1:],
     key=lambda o: (-hops(o[0], o[1]), -o[2]),
 )
+CHIPS = [o for o in PLANE if o[2] == 0]
+GROUP = 4
 DEPTH = sorted(range(1, Z), key=lambda dz: -min(dz, Z - dz))
 
 
@@ -60,8 +62,8 @@
     out_ref,
     res_v, gain_v, q_v, k_v, v_v, nkv_v, lens_s, ow_v, gw_v, uw_v, dw_v,
     row_send, row_recv, col_send, col_recv, side_send, side_recv,
-    proj_send, proj_recv, norm_send, norm_recv, down_send, down_recv, last_send, last_recv,
-    load_sem, send_sem, recv_sem, norm_sem,
+    proj_send, proj_recv, norm_send, norm_recv, pass_recv, pair_send, pair_recv, down_send, down_recv, last_send, last_recv,
+    load_sem, send_sem, recv_sem, norm_sem, pair_sem,
 ):
     kvp = lax.axis_index("kvp")
     z = lax.axis_index("tp")
@@ -198,8 +200,10 @@
     norm_send[:, pl.ds(0, 512)] = (hidden * gain).astype(BF)
     norm_send[:, pl.ds(512, 128)] = jnp.where(low, high, square - high).astype(BF)
 
-    for j, o_ in enumerate(PLANE):
+    n = len(CHIPS)
+    for j, o_ in enumerate(CHIPS):
         send(norm_send, norm_recv.at[j], send_sem.at[4], norm_sem.at[j], (index(o_), z))
+    send(norm_send, pass_recv.at[n], send_sem.at[4], norm_sem.at[2 * n], (index((0, 0, 1)), z))
     for copy in large[1:3]:
         copy.wait()
 
@@ -213,11 +217,22 @@
     gate = jnp.zeros((8, 104), F32)
     up = jnp.zeros((8, 104), F32)
     gate, up, squares = gate_up(norm_send, kvp, gate, up)
-    for j in reversed(range(len(PLANE))):
-        slot = norm_recv.at[j]
-        whole(slot, norm_sem.at[j])
-        gate, up, extra = gate_up(slot, origin(PLANE[j]), gate, up)
-        squares = squares + extra
+    lag = 4
+    for step in range(n + 1 + lag):
+        if step < n:
+            j = n - 1 - step
+            slot = norm_recv.at[j]
+            whole(slot, norm_sem.at[j])
+            send(slot, pass_recv.at[j], send_sem.at[4], norm_sem.at[n + j], (index((0, 0, 1)), z))
+            gate, up, extra = gate_up(slot, origin(CHIPS[j]), gate, up)
+            squares = squares + extra
+        if step >= lag:
+            j = n - (step - lag)
+            slot = pass_recv.at[j]
+            whole(slot, norm_sem.at[n + j])
+            o_ = CHIPS[j] if j < n else (0, 0, 0)
+            gate, up, extra = gate_up(slot, origin((o_[0], o_[1], 1)), gate, up)
+            squares = squares + extra
     squares = squares[:, 0:1] + squares[:, 64:65]
     inverse = lax.rsqrt(squares * (1.0 / D) + EPS)
     gate = gate * inverse
@@ -230,12 +245,24 @@
         cols = pl.ds(pl.multiple_of(block * 512, 512), 512)
         return jnp.dot(inner, dw_v[:, cols], preferred_element_type=F32)
 
-    for j, o_ in enumerate(PLANE):
-        down_send[j] = down(index(o_)).astype(BF)
-        send(down_send.at[j], down_recv.at[j], send_sem.at[5], recv_sem.at[4], (index(o_), z))
-    total = down(kvp)
+    order = CHIPS + [(0, 0, 0)]
+    sibling = (index((0, 0, 1)), z)
+    for g in range(len(order) // GROUP):
+        for j in range(GROUP * g, GROUP * g + GROUP):
+            pair_send[j] = down(index((order[j][0], order[j][1], 1))).astype(BF)
+        slots = pl.ds(GROUP * g, GROUP)
+        send(pair_send.at[slots], pair_recv.at[slots], send_sem.at[5], pair_sem.at[g], sibling)
+    for g in range(len(order) // GROUP):
+        js = range(GROUP * g, GROUP * g + GROUP)
+        blocks = [down(index(order[j])) for j in js]
+        whole(pair_recv.at[pl.ds(GROUP * g, GROUP)], pair_sem.at[g])
+        for j, block in zip(js, blocks):
+            total = block + pair_recv[j].astype(F32)
+            if j < n:
+                down_send[j] = total.astype(BF)
+                send(down_send.at[j], down_recv.at[j], send_sem.at[7], recv_sem.at[4], (index(order[j]), z))
     whole(down_recv, recv_sem.at[4])
-    for j in range(len(PLANE)):
+    for j in range(n):
         total = total + down_recv[j].astype(F32)
 
     for g in range(Z // 2):
@@ -254,33 +281,35 @@
     mine = jnp.where(odd, pltpu.roll(mine, 64, 1), mine)
     out_ref[...] = mine[:, 0:64].astype(BF)
 
-    for i, ref in enumerate((row_recv, side_recv, col_recv, proj_recv, norm_recv, down_recv, last_recv)):
+    for i, ref in enumerate((row_recv, side_recv, col_recv, proj_recv, norm_recv, pair_recv, last_recv, down_recv)):
         whole(ref, send_sem.at[i])
+    whole(pass_recv, send_sem.at[4])
 
 
 def local(residual, norm_gain, queries, keys, values, new_kv, lens, out_weight, gate_weight, up_weight, down_weight):
     V = pltpu.VMEM
-    n = len(PLANE)
+    n = len(CHIPS)
     scratch = [
         V((8, 64), BF), V((64,), BF), V((8, 16, 128), BF), V((8, 128, 128), BF), V((8, 128, 128), BF),
         V((8, 2, 128), BF), pltpu.SMEM((8,), jnp.int32), V((2048, 512), BF),
         V((104, D), BF), V((104, D), BF), V((104, D), BF),
         V((2, 80, 128), BF), V((7, 80, 128), BF), V((80, 128), BF), V((7, 80, 128), BF),
         V((8, 128), BF), V((7, 8, 128), BF),
-        V((8, 512), BF), V((7, 8, 512), BF), V((8, 640), BF), V((n, 8, 640), BF),
+        V((8, 512), BF), V((7, 8, 512), BF), V((8, 640), BF), V((n, 8, 640), BF), V((n + 1, 8, 640), BF),
+        V((n + 1, 8, 512), BF), V((n + 1, 8, 512), BF),
         V((n, 8, 512), BF), V((n, 8, 512), BF), V((4, 8, 128), F32), V((7, 8, 128), F32),
-        pltpu.SemaphoreType.DMA((11,)), pltpu.SemaphoreType.DMA((7,)), pltpu.SemaphoreType.DMA((6,)),
-        pltpu.SemaphoreType.DMA((n,)),
+        pltpu.SemaphoreType.DMA((11,)), pltpu.SemaphoreType.DMA((8,)), pltpu.SemaphoreType.DMA((6,)),
+        pltpu.SemaphoreType.DMA((2 * n + 1,)), pltpu.SemaphoreType.DMA(((n + 1) // GROUP,)),
     ]
     return pl.pallas_call(
         kernel,
         name="decode_step",
         out_shape=jax.ShapeDtypeStruct((8, 64), BF),
-        in_specs=[pl.BlockSpec(memory_space=pl.ANY)] * 11,
+        in_specs=[pl.BlockSpec(memory_space=pltpu.HBM)] * 11,
         out_specs=pl.BlockSpec(memory_space=pltpu.VMEM),
         scratch_shapes=scratch,
         cost_estimate=pl.CostEstimate(flops=120_000_000, bytes_accessed=13_000_000, transcendentals=20_000),
-        compiler_params=pltpu.CompilerParams(collective_id=0, has_side_effects=True, vmem_limit_bytes=48 << 20),
+        compiler_params=pltpu.CompilerParams(collective_id=0, has_side_effects=True, vmem_limit_bytes=60 << 20),
     )(
         residual, norm_gain, queries, keys.reshape(8, 128, 128), values.reshape(8, 128, 128),
         new_kv.reshape(8, 2, 128), lens, out_weight, gate_weight, up_weight, down_weight,

time: 52.3 us -> 43.5 us (0.83)
  local copies, waits for them, and re-layouts: 9.47 us -> 1.26 us
    unnamed x19 -> x1, local copies, waits for them, and re-layouts: 9.47 us -> 1.26 us
where the time goes in v2:
time: 43.5 us; the launch traced here: 43.3 us
  Pallas kernels  42.1 us (97%)
  local copies, waits for them, and re-layouts  1.26 us (3%)
    pallas_call x1, Pallas kernels, local(): pl.pallas_call(kernel, name='decode_step', out_shape=jax.ShapeDtypeStruct...  42.1 us
    unnamed x1, local copies, waits for them, and re-layouts  1.26 us

profile of v2, /device:TPU:1, one launch (start us, length us, event | category | flops | bytes accessed | tf_op | source)
XLA Modules:
  0.0 43.3 jit_solution(15155557175668071955)
XLA Ops:
  0.0 42.1 %decode_step.1 = bf16[8,64]{1,0:T(8,128)(2,1)} custom-call(bf16[8,64]{1,0:T(8,128)(2,1)} %res_h.1, bf16[64]{0:T(256)(128)(2,1)} %gain_h.1, bf16[8,16,128]{2,1,0:T(8,128)(2,1)} %q_h.1, bf16[8,128,128]{2,1,0:T(8,128)(2,1)} %bitcast.3, bf16[8,128,128]{2,1,0:T(8,128)(2,1)} %bitcast.4, bf16[8,2,128]{2,1,0:T(2,128)(2,1)} %bitcast.5, s32[8]{0:T(128)} %lens_h.1, ...), custom_call_target="tpu_custom_call" | custom-call | flops 120000000 | bytes 13000000 | tf_op jit(solution)/shard_map/decode_step/pallas_call | solution.py:304
  42.1 1.3 %copy.13 = bf16[8,64]{1,0:T(8,128)(2,1)} copy(bf16[8,64]{1,0:T(8,128)(2,1)} %decode_step.1) | data formatting | bytes 2048

commit v3 on v2

--- a/solution.py
+++ b/solution.py
@@ -28,9 +28,16 @@
     [(dx, dy, dc) for dx in range(X) for dy in range(Y) for dc in range(C)][1:],
     key=lambda o: (-hops(o[0], o[1]), -o[2]),
 )
+NEAR = [o for o in PLANE if o[2] == 0 and hops(o[0], o[1]) <= 2]
+FAR = [o for o in PLANE if hops(o[0], o[1]) > 2]
+NEAR_SPANS = [(0, 6), (6, 10)]
+FAR_SPANS = [(0, 2), (2, 10)]
+GROUP = 4
 CHIPS = [o for o in PLANE if o[2] == 0]
-GROUP = 4
 DEPTH = sorted(range(1, Z), key=lambda dz: -min(dz, Z - dz))
+GREET = [(dx, 0, dc, 0) for dx in range(X) for dc in range(C)] + [(0, dy, dc, 0) for dy in range(1, Y) for dc in range(C)]
+GREET = GREET[1:] + [(0, 0, 0, dz) for dz in (1, 2, Z - 2, Z - 1)]
+GREET = sorted(GREET, key=lambda o: -hops(o[0], o[1]) - min(o[3], Z - o[3]))
 
 
 def pack(ref, o, m, l):
@@ -62,8 +69,8 @@
     out_ref,
     res_v, gain_v, q_v, k_v, v_v, nkv_v, lens_s, ow_v, gw_v, uw_v, dw_v,
     row_send, row_recv, col_send, col_recv, side_send, side_recv,
-    proj_send, proj_recv, norm_send, norm_recv, pass_recv, pair_send, pair_recv, down_send, down_recv, last_send, last_recv,
-    load_sem, send_sem, recv_sem, norm_sem, pair_sem,
+    proj_send, proj_recv, norm_send, norm_recv, pass_recv, far_recv, pair_send, pair_recv, down_send, down_recv, last_send, last_recv,
+    load_sem, send_sem, recv_sem, norm_sem, pair_sem, side_sem,
 ):
     kvp = lax.axis_index("kvp")
     z = lax.axis_index("tp")
@@ -89,10 +96,8 @@
         copy.start()
 
     barrier = pltpu.get_barrier_semaphore()
-    for dz in DEPTH:
-        pl.semaphore_signal(barrier, inc=1, device_id=(kvp, zs[dz]), device_id_type=MESH)
-    for o in PLANE:
-        pl.semaphore_signal(barrier, inc=1, device_id=(index(o), z), device_id_type=MESH)
+    for o in GREET:
+        pl.semaphore_signal(barrier, inc=1, device_id=(index(o), zs[o[3]]), device_id_type=MESH)
 
     for copy in small:
         copy.wait()
@@ -139,7 +144,7 @@
         [res_v[...], jnp.broadcast_to(gain_v[...].astype(F32).reshape(1, 64), (8, 64)).astype(BF)], axis=1
     )
 
-    pl.semaphore_wait(barrier, len(PLANE) + len(DEPTH))
+    pl.semaphore_wait(barrier, len(GREET))
 
     def send(src, dst, sends, recvs, device):
         pltpu.make_async_remote_copy(src, dst, sends, recvs, device_id=device, device_id_type=MESH).start()
@@ -150,14 +155,23 @@
     for j, o_ in enumerate(ROW):
         send(row_send.at[cs[o_[2]]], row_recv.at[j], send_sem.at[0], recv_sem.at[0], (index(o_), z))
     for j, dz in enumerate(DEPTH):
-        send(side_send, side_recv.at[j], send_sem.at[1], recv_sem.at[1], (kvp, zs[dz]))
+        if min(dz, Z - dz) <= 2:
+            send(side_send, side_recv.at[j], send_sem.at[1], side_sem.at[j], (kvp, zs[dz]))
     whole(row_recv, recv_sem.at[0])
     o, m, l = combine([unpack(row_send[c])] + [unpack(row_recv[j]) for j in range(len(ROW))])
     pack(col_send, o, m, l)
 
     for j, o_ in enumerate(COL):
         send(col_send, col_recv.at[j], send_sem.at[2], recv_sem.at[2], (index(o_), z))
-    whole(side_recv, recv_sem.at[1])
+    for j, dz in enumerate(DEPTH):
+        if min(dz, Z - dz) <= 2:
+            whole(side_recv.at[j], side_sem.at[j])
+    for j, dz in enumerate(DEPTH):
+        if min(dz, Z - dz) > 2:
+            send(side_send, side_recv.at[j], send_sem.at[1], side_sem.at[j], (kvp, zs[dz]))
+    for j, dz in enumerate(DEPTH):
+        if min(dz, Z - dz) > 2:
+            whole(side_recv.at[j], side_sem.at[j])
     lane8 = lax.broadcasted_iota(jnp.int32, (8, 128), 1)
     low = lane8 < 64
     side = [side_send[...].astype(F32)] + [side_recv[j].astype(F32) for j in range(Z - 1)]
@@ -200,10 +214,14 @@
     norm_send[:, pl.ds(0, 512)] = (hidden * gain).astype(BF)
     norm_send[:, pl.ds(512, 128)] = jnp.where(low, high, square - high).astype(BF)
 
-    n = len(CHIPS)
-    for j, o_ in enumerate(CHIPS):
-        send(norm_send, norm_recv.at[j], send_sem.at[4], norm_sem.at[j], (index(o_), z))
-    send(norm_send, pass_recv.at[n], send_sem.at[4], norm_sem.at[2 * n], (index((0, 0, 1)), z))
+    n = len(NEAR)
+    sibling = (index((0, 0, 1)), z)
+    span_of = lambda spans, j: max(k for k, (lo, _) in enumerate(spans) if lo <= j)
+    for j, o_ in enumerate(NEAR):
+        send(norm_send, norm_recv.at[j], send_sem.at[4], norm_sem.at[span_of(NEAR_SPANS, j)], (index(o_), z))
+    for j, o_ in enumerate(FAR):
+        send(norm_send, far_recv.at[j], send_sem.at[8], norm_sem.at[2 + span_of(FAR_SPANS, j)], (index(o_), z))
+    send(norm_send, pass_recv.at[n], send_sem.at[4], norm_sem.at[4], sibling)
     for copy in large[1:3]:
         copy.wait()
 
@@ -217,21 +235,25 @@
     gate = jnp.zeros((8, 104), F32)
     up = jnp.zeros((8, 104), F32)
     gate, up, squares = gate_up(norm_send, kvp, gate, up)
-    lag = 4
-    for step in range(n + 1 + lag):
-        if step < n:
-            j = n - 1 - step
-            slot = norm_recv.at[j]
-            whole(slot, norm_sem.at[j])
-            send(slot, pass_recv.at[j], send_sem.at[4], norm_sem.at[n + j], (index((0, 0, 1)), z))
-            gate, up, extra = gate_up(slot, origin(CHIPS[j]), gate, up)
+    for k, (lo, hi) in reversed(list(enumerate(NEAR_SPANS))):
+        slots = norm_recv.at[pl.ds(lo, hi - lo)]
+        whole(slots, norm_sem.at[k])
+        send(slots, pass_recv.at[pl.ds(lo, hi - lo)], send_sem.at[4], norm_sem.at[5 + k], sibling)
+        for j in reversed(range(lo, hi)):
+            gate, up, extra = gate_up(norm_recv.at[j], origin(NEAR[j]), gate, up)
             squares = squares + extra
-        if step >= lag:
-            j = n - (step - lag)
-            slot = pass_recv.at[j]
-            whole(slot, norm_sem.at[n + j])
-            o_ = CHIPS[j] if j < n else (0, 0, 0)
-            gate, up, extra = gate_up(slot, origin((o_[0], o_[1], 1)), gate, up)
+    whole(pass_recv.at[n], norm_sem.at[4])
+    gate, up, extra = gate_up(pass_recv.at[n], origin((0, 0, 1)), gate, up)
+    squares = squares + extra
+    for k, (lo, hi) in reversed(list(enumerate(NEAR_SPANS))):
+        whole(pass_recv.at[pl.ds(lo, hi - lo)], norm_sem.at[5 + k])
+        for j in reversed(range(lo, hi)):
+            gate, up, extra = gate_up(pass_recv.at[j], origin((NEAR[j][0], NEAR[j][1], 1)), gate, up)
+            squares = squares + extra
+    for k, (lo, hi) in reversed(list(enumerate(FAR_SPANS))):
+        whole(far_recv.at[pl.ds(lo, hi - lo)], norm_sem.at[2 + k])
+        for j in reversed(range(lo, hi)):
+            gate, up, extra = gate_up(far_recv.at[j], origin(FAR[j]), gate, up)
             squares = squares + extra
     squares = squares[:, 0:1] + squares[:, 64:65]
     inverse = lax.rsqrt(squares * (1.0 / D) + EPS)
@@ -245,6 +267,7 @@
         cols = pl.ds(pl.multiple_of(block * 512, 512), 512)
         return jnp.dot(inner, dw_v[:, cols], preferred_element_type=F32)
 
+    n = len(CHIPS)
     order = CHIPS + [(0, 0, 0)]
     sibling = (index((0, 0, 1)), z)
     for g in range(len(order) // GROUP):
@@ -281,25 +304,26 @@
     mine = jnp.where(odd, pltpu.roll(mine, 64, 1), mine)
     out_ref[...] = mine[:, 0:64].astype(BF)
 
-    for i, ref in enumerate((row_recv, side_recv, col_recv, proj_recv, norm_recv, pair_recv, last_recv, down_recv)):
+    for i, ref in enumerate((row_recv, side_recv, col_recv, proj_recv, norm_recv, pair_recv, last_recv, down_recv, far_recv)):
         whole(ref, send_sem.at[i])
     whole(pass_recv, send_sem.at[4])
 
 
 def local(residual, norm_gain, queries, keys, values, new_kv, lens, out_weight, gate_weight, up_weight, down_weight):
     V = pltpu.VMEM
-    n = len(CHIPS)
+    n, far = len(NEAR), len(FAR)
     scratch = [
         V((8, 64), BF), V((64,), BF), V((8, 16, 128), BF), V((8, 128, 128), BF), V((8, 128, 128), BF),
         V((8, 2, 128), BF), pltpu.SMEM((8,), jnp.int32), V((2048, 512), BF),
         V((104, D), BF), V((104, D), BF), V((104, D), BF),
         V((2, 80, 128), BF), V((7, 80, 128), BF), V((80, 128), BF), V((7, 80, 128), BF),
         V((8, 128), BF), V((7, 8, 128), BF),
-        V((8, 512), BF), V((7, 8, 512), BF), V((8, 640), BF), V((n, 8, 640), BF), V((n + 1, 8, 640), BF),
-        V((n + 1, 8, 512), BF), V((n + 1, 8, 512), BF),
-        V((n, 8, 512), BF), V((n, 8, 512), BF), V((4, 8, 128), F32), V((7, 8, 128), F32),
-        pltpu.SemaphoreType.DMA((11,)), pltpu.SemaphoreType.DMA((8,)), pltpu.SemaphoreType.DMA((6,)),
-        pltpu.SemaphoreType.DMA((2 * n + 1,)), pltpu.SemaphoreType.DMA(((n + 1) // GROUP,)),
+        V((8, 512), BF), V((7, 8, 512), BF),
+        V((8, 640), BF), V((n, 8, 640), BF), V((n + 1, 8, 640), BF), V((far, 8, 640), BF),
+        V((16, 8, 512), BF), V((16, 8, 512), BF),
+        V((len(CHIPS), 8, 512), BF), V((len(CHIPS), 8, 512), BF), V((4, 8, 128), F32), V((7, 8, 128), F32),
+        pltpu.SemaphoreType.DMA((11,)), pltpu.SemaphoreType.DMA((9,)), pltpu.SemaphoreType.DMA((6,)),
+        pltpu.SemaphoreType.DMA((7,)), pltpu.SemaphoreType.DMA((4,)), pltpu.SemaphoreType.DMA((Z - 1,)),
     ]
     return pl.pallas_call(
         kernel,

time: 43.5 us -> 42.1 us (0.968)
  Pallas kernels: 42.1 us -> 40.7 us
    pallas_call x1, Pallas kernels: 42.1 us -> 40.7 us  [local(): pl.pallas_call(kernel, name='decode_step', out_shape=jax.ShapeDtypeStruct...]
where the time goes in v3:
time: 42.1 us; the launch traced here: 42 us
  Pallas kernels  40.7 us (97%)
  local copies, waits for them, and re-layouts  1.26 us (3%)
    pallas_call x1, Pallas kernels, local(): pl.pallas_call(kernel, name='decode_step', out_shape=jax.ShapeDtypeStruct...  40.7 us
    unnamed x1, local copies, waits for them, and re-layouts  1.26 us

profile of v3, /device:TPU:1, one launch (start us, length us, event | category | flops | bytes accessed | tf_op | source)
XLA Modules:
  0.0 42.0 jit_solution(3936412677618577030)
XLA Ops:
  0.0 40.7 %decode_step.1 = bf16[8,64]{1,0:T(8,128)(2,1)} custom-call(bf16[8,64]{1,0:T(8,128)(2,1)} %res_h.1, bf16[64]{0:T(256)(128)(2,1)} %gain_h.1, bf16[8,16,128]{2,1,0:T(8,128)(2,1)} %q_h.1, bf16[8,128,128]{2,1,0:T(8,128)(2,1)} %bitcast.3, bf16[8,128,128]{2,1,0:T(8,128)(2,1)} %bitcast.4, bf16[8,2,128]{2,1,0:T(2,128)(2,1)} %bitcast.5, s32[8]{0:T(128)} %lens_h.1, ...), custom_call_target="tpu_custom_call" | custom-call | flops 120000000 | bytes 13000000 | tf_op jit(solution)/shard_map/decode_step/pallas_call | solution.py:328
  40.7 1.3 %copy.13 = bf16[8,64]{1,0:T(8,128)(2,1)} copy(bf16[8,64]{1,0:T(8,128)(2,1)} %decode_step.1) | data formatting | bytes 2048

commit v4 on v3

--- a/solution.py
+++ b/solution.py
@@ -41,16 +41,16 @@
 
 
 def pack(ref, o, m, l):
-    rows = lax.broadcasted_iota(jnp.int32, (16, 128), 0)
+    rows = lax.broadcasted_iota(jnp.int32, (8, 128), 0)
     high = l.astype(BF).astype(F32)
     tail = jnp.where(rows == 0, m, jnp.where(rows == 1, high, jnp.where(rows == 2, l - high, 0.0)))
-    ref[pl.ds(0, 64), :] = o.astype(BF)
-    ref[pl.ds(64, 16), :] = tail.astype(BF)
+    ref[pl.ds(0, 8)] = o.reshape(8, 8, 128).astype(BF)
+    ref[8] = tail.astype(BF)
 
 
 def unpack(x):
-    o = x[0:64].astype(F32)
-    tail = x[64:80].astype(F32)
+    o = x[0:8].astype(F32).reshape(64, 128)
+    tail = x[8].astype(F32)
     return o, tail[0:1], tail[1:2] + tail[2:3]
 
 
@@ -316,7 +316,7 @@
         V((8, 64), BF), V((64,), BF), V((8, 16, 128), BF), V((8, 128, 128), BF), V((8, 128, 128), BF),
         V((8, 2, 128), BF), pltpu.SMEM((8,), jnp.int32), V((2048, 512), BF),
         V((104, D), BF), V((104, D), BF), V((104, D), BF),
-        V((2, 80, 128), BF), V((7, 80, 128), BF), V((80, 128), BF), V((7, 80, 128), BF),
+        V((2, 9, 8, 128), BF), V((7, 9, 8, 128), BF), V((9, 8, 128), BF), V((7, 9, 8, 128), BF),
         V((8, 128), BF), V((7, 8, 128), BF),
         V((8, 512), BF), V((7, 8, 512), BF),
         V((8, 640), BF), V((n, 8, 640), BF), V((n + 1, 8, 640), BF), V((far, 8, 640), BF),

time: 42.1 us -> 41.8 us (level)
  no operation moved by 1% of the time
where the time goes in v4:
time: 41.8 us; the launch traced here: 41.7 us
  Pallas kernels  40.5 us (97%)
  local copies, waits for them, and re-layouts  1.26 us (3%)
    pallas_call x1, Pallas kernels, local(): pl.pallas_call(kernel, name='decode_step', out_shape=jax.ShapeDtypeStruct...  40.5 us
    unnamed x1, local copies, waits for them, and re-layouts  1.26 us

profile of v4, /device:TPU:1, one launch (start us, length us, event | category | flops | bytes accessed | tf_op | source)
XLA Modules:
  0.0 41.7 jit_solution(721964179858055652)
XLA Ops:
  0.0 40.5 %decode_step.1 = bf16[8,64]{1,0:T(8,128)(2,1)} custom-call(bf16[8,64]{1,0:T(8,128)(2,1)} %res_h.1, bf16[64]{0:T(256)(128)(2,1)} %gain_h.1, bf16[8,16,128]{2,1,0:T(8,128)(2,1)} %q_h.1, bf16[8,128,128]{2,1,0:T(8,128)(2,1)} %bitcast.3, bf16[8,128,128]{2,1,0:T(8,128)(2,1)} %bitcast.4, bf16[8,2,128]{2,1,0:T(2,128)(2,1)} %bitcast.5, s32[8]{0:T(128)} %lens_h.1, ...), custom_call_target="tpu_custom_call" | custom-call | flops 120000000 | bytes 13000000 | tf_op jit(solution)/shard_map/decode_step/pallas_call | solution.py:328
  40.5 1.3 %copy.13 = bf16[8,64]{1,0:T(8,128)(2,1)} copy(bf16[8,64]{1,0:T(8,128)(2,1)} %decode_step.1) | data formatting | bytes 2048

commit v5 on v4

--- a/solution.py
+++ b/solution.py
@@ -31,8 +31,8 @@
 NEAR = [o for o in PLANE if o[2] == 0 and hops(o[0], o[1]) <= 2]
 FAR = [o for o in PLANE if hops(o[0], o[1]) > 2]
 NEAR_SPANS = [(0, 6), (6, 10)]
-FAR_SPANS = [(0, 2), (2, 10)]
-GROUP = 4
+FAR_SPANS = [(0, 10)]
+GROUP = 8
 CHIPS = [o for o in PLANE if o[2] == 0]
 DEPTH = sorted(range(1, Z), key=lambda dz: -min(dz, Z - dz))
 GREET = [(dx, 0, dc, 0) for dx in range(X) for dc in range(C)] + [(0, dy, dc, 0) for dy in range(1, Y) for dc in range(C)]
@@ -156,22 +156,18 @@
         send(row_send.at[cs[o_[2]]], row_recv.at[j], send_sem.at[0], recv_sem.at[0], (index(o_), z))
     for j, dz in enumerate(DEPTH):
         if min(dz, Z - dz) <= 2:
-            send(side_send, side_recv.at[j], send_sem.at[1], side_sem.at[j], (kvp, zs[dz]))
+            send(side_send, side_recv.at[j], send_sem.at[0], side_sem.at[0], (kvp, zs[dz]))
     whole(row_recv, recv_sem.at[0])
     o, m, l = combine([unpack(row_send[c])] + [unpack(row_recv[j]) for j in range(len(ROW))])
     pack(col_send, o, m, l)
 
     for j, o_ in enumerate(COL):
-        send(col_send, col_recv.at[j], send_sem.at[2], recv_sem.at[2], (index(o_), z))
-    for j, dz in enumerate(DEPTH):
-        if min(dz, Z - dz) <= 2:
-            whole(side_recv.at[j], side_sem.at[j])
+        send(col_send, col_recv.at[j], send_sem.at[0], recv_sem.at[2], (index(o_), z))
+    whole(side_recv.at[pl.ds(3, 4)], side_sem.at[0])
     for j, dz in enumerate(DEPTH):
         if min(dz, Z - dz) > 2:
-            send(side_send, side_recv.at[j], send_sem.at[1], side_sem.at[j], (kvp, zs[dz]))
-    for j, dz in enumerate(DEPTH):
-        if min(dz, Z - dz) > 2:
-            whole(side_recv.at[j], side_sem.at[j])
+            send(side_send, side_recv.at[j], send_sem.at[0], side_sem.at[1], (kvp, zs[dz]))
+    whole(side_recv.at[pl.ds(0, 3)], side_sem.at[1])
     lane8 = lax.broadcasted_iota(jnp.int32, (8, 128), 1)
     low = lane8 < 64
     side = [side_send[...].astype(F32)] + [side_recv[j].astype(F32) for j in range(Z - 1)]
@@ -203,7 +199,7 @@
     part = jnp.dot(att, ow_v[...], preferred_element_type=F32)
     proj_send[...] = part.astype(BF)
     for j, dz in enumerate(DEPTH):
-        send(proj_send, proj_recv.at[j], send_sem.at[3], recv_sem.at[3], (kvp, zs[dz]))
+        send(proj_send, proj_recv.at[j], send_sem.at[0], recv_sem.at[3], (kvp, zs[dz]))
     whole(proj_recv, recv_sem.at[3])
     total = part
     for j in range(Z - 1):
@@ -218,10 +214,10 @@
     sibling = (index((0, 0, 1)), z)
     span_of = lambda spans, j: max(k for k, (lo, _) in enumerate(spans) if lo <= j)
     for j, o_ in enumerate(NEAR):
-        send(norm_send, norm_recv.at[j], send_sem.at[4], norm_sem.at[span_of(NEAR_SPANS, j)], (index(o_), z))
+        send(norm_send, norm_recv.at[j], send_sem.at[0], norm_sem.at[span_of(NEAR_SPANS, j)], (index(o_), z))
     for j, o_ in enumerate(FAR):
-        send(norm_send, far_recv.at[j], send_sem.at[8], norm_sem.at[2 + span_of(FAR_SPANS, j)], (index(o_), z))
-    send(norm_send, pass_recv.at[n], send_sem.at[4], norm_sem.at[4], sibling)
+        send(norm_send, far_recv.at[j], send_sem.at[0], norm_sem.at[2 + span_of(FAR_SPANS, j)], (index(o_), z))
+    send(norm_send, pass_recv.at[n], send_sem.at[0], norm_sem.at[3], sibling)
     for copy in large[1:3]:
         copy.wait()
 
@@ -238,15 +234,15 @@
     for k, (lo, hi) in reversed(list(enumerate(NEAR_SPANS))):
         slots = norm_recv.at[pl.ds(lo, hi - lo)]
         whole(slots, norm_sem.at[k])
-        send(slots, pass_recv.at[pl.ds(lo, hi - lo)], send_sem.at[4], norm_sem.at[5 + k], sibling)
+        send(slots, pass_recv.at[pl.ds(lo, hi - lo)], send_sem.at[0], norm_sem.at[4 + k], sibling)
         for j in reversed(range(lo, hi)):
             gate, up, extra = gate_up(norm_recv.at[j], origin(NEAR[j]), gate, up)
             squares = squares + extra
-    whole(pass_recv.at[n], norm_sem.at[4])
+    whole(pass_recv.at[n], norm_sem.at[3])
     gate, up, extra = gate_up(pass_recv.at[n], origin((0, 0, 1)), gate, up)
     squares = squares + extra
     for k, (lo, hi) in reversed(list(enumerate(NEAR_SPANS))):
-        whole(pass_recv.at[pl.ds(lo, hi - lo)], norm_sem.at[5 + k])
+        whole(pass_recv.at[pl.ds(lo, hi - lo)], norm_sem.at[4 + k])
         for j in reversed(range(lo, hi)):
             gate, up, extra = gate_up(pass_recv.at[j], origin((NEAR[j][0], NEAR[j][1], 1)), gate, up)
             squares = squares + extra
@@ -274,7 +270,7 @@
         for j in range(GROUP * g, GROUP * g + GROUP):
             pair_send[j] = down(index((order[j][0], order[j][1], 1))).astype(BF)
         slots = pl.ds(GROUP * g, GROUP)
-        send(pair_send.at[slots], pair_recv.at[slots], send_sem.at[5], pair_sem.at[g], sibling)
+        send(pair_send.at[slots], pair_recv.at[slots], send_sem.at[0], pair_sem.at[g], sibling)
     for g in range(len(order) // GROUP):
         js = range(GROUP * g, GROUP * g + GROUP)
         blocks = [down(index(order[j])) for j in js]
@@ -283,7 +279,7 @@
             total = block + pair_recv[j].astype(F32)
             if j < n:
                 down_send[j] = total.astype(BF)
-                send(down_send.at[j], down_recv.at[j], send_sem.at[7], recv_sem.at[4], (index(order[j]), z))
+                send(down_send.at[j], down_recv.at[j], send_sem.at[0], recv_sem.at[4], (index(order[j]), z))
     whole(down_recv, recv_sem.at[4])
     for j in range(n):
         total = total + down_recv[j].astype(F32)
@@ -291,12 +287,12 @@
     for g in range(Z // 2):
         last_send[g] = total[:, 128 * g : 128 * g + 128]
     for j, dz in enumerate(DEPTH):
-        send(last_send.at[zs[dz] // 2], last_recv.at[j], send_sem.at[6], recv_sem.at[5], (kvp, zs[dz]))
+        send(last_send.at[zs[dz] // 2], last_recv.at[j], send_sem.at[0], recv_sem.at[1], (kvp, zs[dz]))
     mine = last_send[z // 2]
     hid = jnp.zeros((8, 128), F32)
     for g in range(Z // 2):
         hid = jnp.where((jnp.zeros((8, 128), jnp.int32) + z // 2) == g, hidden[:, 128 * g : 128 * g + 128], hid)
-    whole(last_recv, recv_sem.at[5])
+    whole(last_recv, recv_sem.at[1])
     for j in range(Z - 1):
         mine = mine + last_recv[j]
     mine = mine + hid
@@ -304,9 +300,9 @@
     mine = jnp.where(odd, pltpu.roll(mine, 64, 1), mine)
     out_ref[...] = mine[:, 0:64].astype(BF)
 
-    for i, ref in enumerate((row_recv, side_recv, col_recv, proj_recv, norm_recv, pair_recv, last_recv, down_recv, far_recv)):
-        whole(ref, send_sem.at[i])
-    whole(pass_recv, send_sem.at[4])
+    for ref in (row_recv, side_recv, col_recv, proj_recv, norm_recv, pair_recv, last_recv, down_recv, far_recv):
+        whole(ref, send_sem.at[0])
+    whole(pass_recv, send_sem.at[0])
 
 
 def local(residual, norm_gain, queries, keys, values, new_kv, lens, out_weight, gate_weight, up_weight, down_weight):
@@ -322,8 +318,8 @@
         V((8, 640), BF), V((n, 8, 640), BF), V((n + 1, 8, 640), BF), V((far, 8, 640), BF),
         V((16, 8, 512), BF), V((16, 8, 512), BF),
         V((len(CHIPS), 8, 512), BF), V((len(CHIPS), 8, 512), BF), V((4, 8, 128), F32), V((7, 8, 128), F32),
-        pltpu.SemaphoreType.DMA((11,)), pltpu.SemaphoreType.DMA((9,)), pltpu.SemaphoreType.DMA((6,)),
-        pltpu.SemaphoreType.DMA((7,)), pltpu.SemaphoreType.DMA((4,)), pltpu.SemaphoreType.DMA((Z - 1,)),
+        pltpu.SemaphoreType.DMA((11,)), pltpu.SemaphoreType.DMA((1,)), pltpu.SemaphoreType.DMA((5,)),
+        pltpu.SemaphoreType.DMA((6,)), pltpu.SemaphoreType.DMA((2,)), pltpu.SemaphoreType.DMA((2,)),
     ]
     return pl.pallas_call(
         kernel,

time: 41.8 us -> 41.7 us (level)
  no operation moved by 1% of the time
where the time goes in v5:
time: 41.7 us; the launch traced here: 41.6 us
  Pallas kernels  40.3 us (97%)
  local copies, waits for them, and re-layouts  1.26 us (3%)
    pallas_call x1, Pallas kernels, local(): pl.pallas_call(kernel, name='decode_step', out_shape=jax.ShapeDtypeStruct...  40.3 us
    unnamed x1, local copies, waits for them, and re-layouts  1.26 us

profile of v5, /device:TPU:1, one launch (start us, length us, event | category | flops | bytes accessed | tf_op | source)
XLA Modules:
  0.0 41.6 jit_solution(17885702539420671683)
XLA Ops:
  0.0 40.3 %decode_step.1 = bf16[8,64]{1,0:T(8,128)(2,1)} custom-call(bf16[8,64]{1,0:T(8,128)(2,1)} %res_h.1, bf16[64]{0:T(256)(128)(2,1)} %gain_h.1, bf16[8,16,128]{2,1,0:T(8,128)(2,1)} %q_h.1, bf16[8,128,128]{2,1,0:T(8,128)(2,1)} %bitcast.3, bf16[8,128,128]{2,1,0:T(8,128)(2,1)} %bitcast.4, bf16[8,2,128]{2,1,0:T(2,128)(2,1)} %bitcast.5, s32[8]{0:T(128)} %lens_h.1, ...), custom_call_target="tpu_custom_call" | custom-call | flops 120000000 | bytes 13000000 | tf_op jit(solution)/shard_map/decode_step/pallas_call | solution.py:324
  40.4 1.3 %copy.13 = bf16[8,64]{1,0:T(8,128)(2,1)} copy(bf16[8,64]{1,0:T(8,128)(2,1)} %decode_step.1) | data formatting | bytes 2048
